TPU v7x, 32 devices: a whole 2x2x4 slice. The times are simulated.
32 devices in a mesh: groups: 2 (over x), rows: 16 (over z, y, core).
Axes of the slice: x: 2, y: 2, z: 4, core: 2. Of those that a mesh axis runs over, the one named last changes fastest.
Arguments:
- features: bfloat16 [128, 4, 3072], P(('groups', 'rows')), parts along dimension 0, may hold values from -6 to 6
- cotangent: bfloat16 [128, 4, 3072], P(('groups', 'rows')), parts along dimension 0, may hold values from -6 to 6
- depth_kernel: float32 [7, 7, 3072], replicated, may hold values from -0.875 to 0.875
- depth_bias: float32 [3072], replicated, may hold values from -3 to 3
- norm_gain: float32 [3072], replicated, may hold values from 0.1 to 1.9
- norm_shift: float32 [3072], replicated, may hold values from -3 to 3
- up_weight: bfloat16 [3072, 12288], P(None, 'rows'), may hold values from -0.109375 to 0.109375
- up_bias: float32 [12288], P('rows'), may hold values from -3 to 3
- down_weight: bfloat16 [12288, 3072], P('rows'), may hold values from -0.109375 to 0.109375
- layer_scale: float32 [3072], replicated, may hold values from 0.3 to 3
Outputs:
- input_grad: bfloat16 [128, 4, 3072], P(('groups', 'rows')), parts along dimension 0
- up_grad: float32 [6144, 12288], P('groups', 'rows'), parts along dimension 0
- up_bias_grad: float32 [24576], P(('groups', 'rows')), parts along dimension 0
- down_grad: float32 [24576, 3072], P(('groups', 'rows')), parts along dimension 0
- kernel_grad: float32 [14, 7, 3072], P('groups'), parts along dimension 0
- depth_bias_grad: float32 [6144], P('groups'), parts along dimension 0
- gain_grad: float32 [6144], P('groups'), parts along dimension 0
- shift_grad: float32 [6144], P('groups'), parts along dimension 0
There are 2 independent parts, one for each index of `groups`. A program takes and returns all parts, laid end to end along the dimension named above; an argument that names none is the same for every part. Nothing has to cross between parts.
All inputs are finite; a program needn't handle non-finite values.
Results may differ from a plain program's by a relative error of at most 0.0075.
Values may be sent and summed in bfloat16 or wider, within the bound.
No kernel may reach another device: no remote copies, remote signals or barrier semaphores. Data moves between devices by JAX's collectives and lax.ppermute only.
A program may use at most 128 MiB of HBM per device.

v0:
```python
import jax
import jax.numpy as jnp
from jax import lax
from jax.sharding import PartitionSpec as P

IMG_ROWS = 32


def extended(cells, sides, width):
    for axis, dim in sides:
        count = lax.axis_size(axis)
        head = lax.slice_in_dim(cells, 0, width, axis=dim)
        tail = lax.slice_in_dim(cells, cells.shape[dim] - width, cells.shape[dim], axis=dim)
        cells = jnp.concatenate(
            [
                lax.ppermute(tail, axis, [(i, (i + 1) % count) for i in range(count)]),
                cells,
                lax.ppermute(head, axis, [((i + 1) % count, i) for i in range(count)]),
            ],
            axis=dim,
        )
    return cells


def gelu_value(pre_act):
    return 0.5 * pre_act * (1.0 + jax.scipy.special.erf(pre_act * 0.7071067811865476))


def gelu_slope(pre_act):
    cdf_part = 0.5 * (1.0 + jax.scipy.special.erf(pre_act * 0.7071067811865476))
    return cdf_part + pre_act * jnp.exp(-0.5 * pre_act * pre_act) * 0.3989422804014327


def contract(left, right, left_dim, right_dim):
    return lax.dot_general(
        left, right, (((left_dim,), (right_dim,)), ((), ())), preferred_element_type=jnp.float32
    )


def depthwise(padded, kernel, offset_term, row_count, col_count):
    summed = jnp.zeros(padded[..., 3 : 3 + row_count, 3 : 3 + col_count, :].shape, padded.dtype)
    for tap_row in range(7):
        for tap_col in range(7):
            summed = (
                summed
                + kernel[tap_row, tap_col]
                * padded[..., tap_row : tap_row + row_count, tap_col : tap_col + col_count, :]
            )
    return summed + offset_term


def depthwise_back(padded_grad, kernel, row_count, col_count):
    summed = jnp.zeros(
        padded_grad[..., 3 : 3 + row_count, 3 : 3 + col_count, :].shape, padded_grad.dtype
    )
    for tap_row in range(7):
        for tap_col in range(7):
            summed = (
                summed
                + kernel[tap_row, tap_col]
                * padded_grad[
                    ...,
                    6 - tap_row : 6 - tap_row + row_count,
                    6 - tap_col : 6 - tap_col + col_count,
                    :,
                ]
            )
    return summed


def normalize(conv_out):
    row_mean = jnp.mean(conv_out, axis=-1, keepdims=True)
    centred = conv_out - row_mean
    inv_std = lax.rsqrt(jnp.mean(centred * centred, axis=-1, keepdims=True) + 1e-06)
    return (centred * inv_std, inv_std)


def norm_back(norm_grad, unit_norm, inv_std, norm_gain):
    scaled = norm_grad * norm_gain
    return inv_std * (
        scaled
        - jnp.mean(scaled, axis=-1, keepdims=True)
        - unit_norm * jnp.mean(scaled * unit_norm, axis=-1, keepdims=True)
    )


def pad_columns(block):
    return jnp.pad(block, ((0, 0), (3, 3), (0, 0)))


def on_device(
    features,
    cotangent,
    depth_kernel,
    depth_bias,
    norm_gain,
    norm_shift,
    up_weight,
    up_bias,
    down_weight,
    layer_scale,
):
    rows_dev, col_count, channels = features.shape
    total_rows = rows_dev * lax.axis_size("rows")
    half_image = IMG_ROWS // 2
    my_index = lax.axis_index("rows")
    first_row = my_index * rows_dev
    row_offsets = first_row - 3 + jnp.arange(rows_dev + 6, dtype=jnp.int32)
    row_image = jnp.mod(row_offsets - half_image, total_rows) // IMG_ROWS
    own_image = jnp.mod(first_row - half_image, total_rows) // IMG_ROWS
    row_mask = (row_image == own_image).astype(jnp.float32)[:, None, None]
    cot_scaled = (
        (cotangent.astype(jnp.float32) * layer_scale)
        .astype(jnp.bfloat16)
        .reshape(rows_dev * col_count, channels)
    )
    cot_all = lax.all_gather(cot_scaled, "rows", axis=0, tiled=True)
    near_rows = extended(features, (("rows", 0),), 3)
    padded = pad_columns(near_rows.astype(jnp.float32) * row_mask)
    conv_out = depthwise(padded, depth_kernel, depth_bias, rows_dev, col_count)
    unit_norm, inv_std = normalize(conv_out)
    normed = (
        (unit_norm * norm_gain + norm_shift)
        .astype(jnp.bfloat16)
        .reshape(rows_dev * col_count, channels)
    )
    normed_all = lax.all_gather(normed, "rows", axis=0, tiled=True)
    pre_act = jnp.dot(normed_all, up_weight, preferred_element_type=jnp.float32) + up_bias
    hidden = gelu_value(pre_act).astype(jnp.bfloat16)
    down_grad = contract(hidden, cot_all, 0, 0)
    hid_grad = contract(cot_all, down_weight, 1, 1)
    act_grad = (hid_grad * gelu_slope(pre_act)).astype(jnp.bfloat16)
    up_bias_grad = jnp.sum(act_grad.astype(jnp.float32), axis=0)
    up_grad = contract(normed_all, act_grad, 0, 0)
    norm_grad = lax.psum_scatter(
        contract(act_grad, up_weight, 1, 1), "rows", scatter_dimension=0, tiled=True
    ).reshape(rows_dev, col_count, channels)
    gain_part = jnp.sum(norm_grad * unit_norm, axis=(0, 1))
    shift_part = jnp.sum(norm_grad, axis=(0, 1))
    conv_grad = norm_back(norm_grad, unit_norm, inv_std, norm_gain)
    bias_part = jnp.sum(conv_grad, axis=(0, 1))
    kernel_rows = []
    for tap_row in range(7):
        kernel_cols = []
        for tap_col in range(7):
            kernel_cols.append(
                jnp.sum(
                    conv_grad
                    * padded[tap_row : tap_row + rows_dev, tap_col : tap_col + col_count, :],
                    axis=(0, 1),
                )
            )
        kernel_rows.append(jnp.stack(kernel_cols))
    kernel_part = jnp.stack(kernel_rows)
    near_grad = extended(conv_grad.astype(jnp.bfloat16), (("rows", 0),), 3).astype(conv_grad.dtype)
    grad_padded = pad_columns(near_grad * row_mask)
    back_term = depthwise_back(grad_padded, depth_kernel, rows_dev, col_count)
    input_grad = (cotangent.astype(jnp.float32) + back_term).astype(jnp.bfloat16)
    gain_grad, shift_grad, kernel_grad, depth_bias_grad = lax.psum(
        (gain_part, shift_part, kernel_part, bias_part), "rows"
    )
    return (
        input_grad,
        up_grad,
        up_bias_grad,
        down_grad,
        kernel_grad,
        depth_bias_grad,
        gain_grad,
        shift_grad,
    )


def solution(mesh):
    in_specs = (
        P(("groups", "rows"), None, None),
        P(("groups", "rows"), None, None),
        P(),
        P(),
        P(),
        P(),
        P(None, "rows"),
        P("rows"),
        P("rows", None),
        P(),
    )
    out_specs = (
        P(("groups", "rows"), None, None),
        P("groups", "rows"),
        P(("groups", "rows")),
        P(("groups", "rows"), None),
        P("groups", None, None),
        P("groups"),
        P("groups"),
        P("groups"),
    )
    return jax.shard_map(
        on_device, mesh=mesh, in_specs=in_specs, out_specs=out_specs, check_vma=False
    )
```

profile of v0, /device:TPU:0, one launch (start us, length us, event | category | flops | bytes accessed | tf_op | source)
XLA Modules:
  0.0 296.4 jit_solution(8445374431140622717)
XLA Ops:
  7.2 0.0 all-gather.5.cloned.1.call-start
  7.2 1.0 fusion.107
  8.2 0.5 collective-permute-start
  8.7 5.1 %collective-permute-start.1 = (bf16[3,4,3072]{2,1,0:T(4,128)(2,1)S(1)}, bf16[3,4,3072]{2,1,0:T(4,128)(2,1)S(1)}, u32[]{:S(2)}, u32[]{:S(2)}) collective-permute-start(bf16[3,4,3072]{2,1,0:T(4,128)(2,1)S(1)} %get-tuple-element.121), channel_id=1, source_target_pairs={{1,0},{2,1},{3,2},{4,3},{5,4},{6,5},{7,6},{8,7},{9,8},{10,9},{11,1... | collective-permute-start | bytes 221192 | tf_op jit(solution)/shard_map/ppermute | solution.py:18
  13.8 1.7 fusion.105
  15.6 2.3 fusion.103
  17.9 0.0 copy-start.27
  18.1 2.8 fusion.104
  20.9 0.0 copy-start.4
  21.0 0.0 copy-start.86
  21.0 0.6 compare_convert_fusion
  21.6 0.0 collective-permute-done
  21.6 0.0 collective-permute-done.1
  21.6 1.1 convert_multiply_fusion.1
  22.7 0.0 copy-start.3
  22.7 0.0 copy-start.87
  22.7 0.0 copy-start.88
  22.7 5.2 %fusion.102 = (f32[4,4]{1,0:T(4,128)S(1)}, f32[4,4,3072]{2,1,0:T(4,128)S(1)}) fusion(f32[3072]{0:T(1024)S(1)} %copy-done.85, f32[3072]{0:T(1024)S(1)} %bitcast.139, f32[3072]{0:T(1024)S(1)} %bitcast.141, f32[3072]{0:T(1024)S(1)} %bitcast.145, f32[10,4,3072]{2,1,0:T(4,128)S(1)} %convert_multiply_fusion.1, f32[3072]{0:T(1024)S(1)} %bitcast.147, ...), kind=kLoop, calls=%fused_computation.279 | loop fusion | flops 4866032 | bytes 2678848 | tf_op jit(solution)/shard_map/reduce_sum | solution.py:72
  28.3 0.2 multiply_reduce_fusion.52
  28.5 0.0 copy-start.83
  28.5 0.1 add_convert_fusion
  28.8 0.7 reshape.90
  29.4 0.0 all-gather.5.cloned.1.call-update
  29.5 0.0 all-gather.3.cloned.1.call-start
  29.6 0.7 reshape.89
  30.2 0.0 all-gather.3.cloned.1.call-update
  30.3 0.0 reduce-scatter.2.cloned.1.call-start
  30.3 37.9 %all-gather.5.cloned.1.call-done = bf16[256,3072]{1,0:T(8,128)(2,1)} async-done(((bf16[16,3072]{1,0:T(8,128)(2,1)}), bf16[256,3072]{1,0:T(8,128)(2,1)}) %all-gather.5.cloned.1.call-update) | async-done | bytes 1572880 | tf_op jit(solution)/shard_map/all_gather | solution.py:127
  68.2 4.2 %convolution_add_fusion = f32[256,768]{1,0:T(8,128)S(1)} fusion(bf16[256,3072]{1,0:T(8,128)(2,1)} %all-gather.5.cloned.1.call-done, bf16[3072,768]{1,0:T(8,128)(2,1)} %param.16, f32[768]{0:T(1024)S(1)} %copy-done.88), kind=kOutput, calls=%fused_computation.85 | convolution fusion | flops 1208156160 | bytes 7080960 | tf_op jit(solution)/shard_map/dot_general | solution.py:128
  72.4 37.2 %all-gather.3.cloned.1.call-done = bf16[256,3072]{1,0:T(8,128)(2,1)} async-done(((bf16[16,3072]{1,0:T(8,128)(2,1)}), bf16[256,3072]{1,0:T(8,128)(2,1)}) %all-gather.3.cloned.1.call-update) | async-done | bytes 1572880 | tf_op jit(solution)/shard_map/all_gather | solution.py:117
  109.7 5.0 %convert_reduce_fusion = (f32[768]{0:T(1024)}, bf16[256,768]{1,0:T(8,128)(2,1)S(1)}) fusion(f32[256,768]{1,0:T(8,128)S(1)} %convolution_add_fusion, bf16[256,3072]{1,0:T(8,128)(2,1)} %all-gather.3.cloned.1.call-done, bf16[768,3072]{1,0:T(8,128)(2,1)} %param.18), kind=kOutput, calls=%fused_computation.93 | convolution fusion | flops 1210318080 | bytes 7474176 | tf_op jit(solution)/shard_map/dot_general | solution.py:35
  114.6 5.4 %fusion.108 = f32[256,3072]{1,0:T(8,128)} fusion(bf16[256,768]{1,0:T(8,128)(2,1)S(1)} %get-tuple-element.123, bf16[3072,768]{1,0:T(8,128)(2,1)} %param.16), kind=kOutput, calls=%fused_computation.285 | convolution fusion | flops 1207959552 | bytes 8257536 | tf_op jit(solution)/shard_map/dot_general | solution.py:35
  120.1 0.0 reduce-scatter.2.cloned.1.call-update
  120.1 0.2 all-reduce.5.cloned.1.call-start
  120.3 1.2 copy-done
  121.5 5.2 %fusion.109 = f32[3072,768]{1,0:T(8,128)} fusion(bf16[256,3072]{1,0:T(8,128)(2,1)S(1)} %copy-done, bf16[256,768]{1,0:T(8,128)(2,1)S(1)} %get-tuple-element.123), kind=kOutput, calls=%fused_computation.286 | convolution fusion | flops 1207959552 | bytes 11403264 | tf_op jit(solution)/shard_map/dot_general | solution.py:35
  126.7 5.2 %fusion.5 = f32[768,3072]{1,0:T(8,128)} fusion(bf16[256,3072]{1,0:T(8,128)(2,1)S(1)} %copy-done.1, f32[256,768]{1,0:T(8,128)S(1)} %convolution_add_fusion), kind=kOutput, calls=%fused_computation.97 | convolution fusion | flops 1208942592 | bytes 11796480 | tf_op jit(solution)/shard_map/dot_general | solution.py:35
  131.9 53.5 %reduce-scatter.2.cloned.1.call-done = f32[16,3072]{1,0:T(8,128)} async-done(((f32[256,3072]{1,0:T(8,128)}), f32[16,3072]{1,0:T(8,128)}) %reduce-scatter.2.cloned.1.call-update) | async-done | bytes 196624 | tf_op jit(solution)/shard_map/reduce_scatter | solution.py:135
  185.4 1.1 fusion.101
  186.4 0.1 div.44
  186.5 1.0 reshape.91
  187.5 0.3 multiply_reduce_fusion
  187.8 1.5 multiply_reduce_fusion.1
  189.3 1.0 multiply_reduce_fusion.37
  190.3 1.3 multiply_reduce_fusion.19
  191.7 0.1 collective-permute-start.2
  191.8 4.4 %collective-permute-start.3 = (bf16[3,4,3072]{2,1,0:T(4,128)(2,1)S(1)}, bf16[3,4,3072]{2,1,0:T(4,128)(2,1)S(1)}, u32[]{:S(2)}, u32[]{:S(2)}) collective-permute-start(bf16[3,4,3072]{2,1,0:T(4,128)(2,1)S(1)} %get-tuple-element.119), channel_id=1, source_target_pairs={{1,0},{2,1},{3,2},{4,3},{5,4},{6,5},{7,6},{8,7},{9,8},{10,9},{11,1... | collective-permute-start | bytes 221192 | tf_op jit(solution)/shard_map/ppermute | solution.py:18
  196.2 0.1 stack.199
  196.7 0.1 stack.208
  196.9 0.1 stack.217
  197.1 0.1 stack.226
  197.2 0.1 stack.235
  197.4 0.1 stack.244
  197.5 0.1 stack.253
  197.7 0.0 copy-start.2
  197.7 0.8 copy-done.2
  198.5 0.0 all-reduce.5.cloned.1.call-update
  198.6 58.5 %all-reduce.2 = (f32[3072]{0:T(1024)}, f32[3072]{0:T(1024)}, f32[3072]{0:T(1024)}) all-reduce(f32[3072]{0:T(1024)S(1)} %get-tuple-element.61, f32[3072]{0:T(1024)S(1)} %get-tuple-element.57, f32[3072]{0:T(1024)S(1)} %get-tuple-element.59), channel_id=1, replica_groups=mesh['groups'=2,'rows'=16] {'rows'}, use_global_device_ids=true, to_apply=%region_57.58 | all-reduce | flops 9216 | bytes 73728 | tf_op jit(solution)/shard_map/psum | solution.py:159
  257.1 0.0 collective-permute-done.2
  257.1 0.0 collective-permute-done.3
  257.1 0.9 convert_multiply_fusion
  258.3 4.2 %fusion.8 = bf16[4,4,3072]{2,1,0:T(4,128)(2,1)} fusion(bf16[4,4,3072]{2,1,0:T(4,128)(2,1)S(1)} %copy-done.3, f32[10,4,3072]{2,1,0:T(4,128)S(1)} %convert_multiply_fusion, f32[3072]{0:T(1024)S(1)} %bitcast.140, f32[3072]{0:T(1024)S(1)} %bitcast.142, f32[3072]{0:T(1024)S(1)} %bitcast.146, f32[3072]{0:T(1024)S(1)} %bitcast.148, f32[3072]{0:T(1024)S(1)} %bitcast.150, ...), kind=kLoop, calls=%fused_computation.102 | loop fusion | flops 4915200 | bytes 2666496 | tf_op jit(solution)/shard_map/convert_element_type | solution.py:158
  262.6 25.3 %all-reduce.5.cloned.1.call-done = f32[7,7,3072]{2,1,0:T(8,128)} async-done(((f32[7,7,3072]{2,1,0:T(8,128)}), f32[7,7,3072]{2,1,0:T(8,128)}) %all-reduce.5.cloned.1.call-update) | async-done | bytes 602128 | tf_op jit(solution)/shard_map/psum | solution.py:159
  287.9 2.0 copy.25
  (181 shorter events, 0.5 us)
Async XLA Ops:
  7.2 15.5 %copy-start.85 = (f32[3072]{0:T(1024)S(1)}, f32[3072]{0:T(1024)}, u32[]{:S(2)}) copy-start(f32[3072]{0:T(1024)} %param.13) | copy-start | bytes 36868
  7.2 61.0 %all-gather.5.cloned.1.call-start = ((), (), s32[]{:S(2)}) async-start(), calls=%async_computation.2 | async-start | bytes 1671168 | tf_op jit(solution)/shard_map/all_gather | solution.py:127
  8.2 13.4 %collective-permute-start = (bf16[3,4,3072]{2,1,0:T(4,128)(2,1)S(1)}, bf16[3,4,3072]{2,1,0:T(4,128)(2,1)S(1)}, u32[]{:S(2)}, u32[]{:S(2)}) collective-permute-start(bf16[3,4,3072]{2,1,0:T(4,128)(2,1)S(1)} %get-tuple-element.120), channel_id=1, source_target_pairs={{0,1},{1,2},{2,3},{3,4},{4,5},{5,6},{6,7},{7,8},{8,9},{9,10},{10,1... | collective-permute-start | bytes 221192 | tf_op jit(solution)/shard_map/ppermute | solution.py:16
  8.7 12.9 %collective-permute-start.1 = (bf16[3,4,3072]{2,1,0:T(4,128)(2,1)S(1)}, bf16[3,4,3072]{2,1,0:T(4,128)(2,1)S(1)}, u32[]{:S(2)}, u32[]{:S(2)}) collective-permute-start(bf16[3,4,3072]{2,1,0:T(4,128)(2,1)S(1)} %get-tuple-element.121), channel_id=1, source_target_pairs={{1,0},{2,1},{3,2},{4,3},{5,4},{6,5},{7,6},{8,7},{9,8},{10,9},{11,1... | collective-permute-start | bytes 221192 | tf_op jit(solution)/shard_map/ppermute | solution.py:18
  15.5 12.5 %copy-start.5 = (f32[1,1,3072]{2,1,0:T(1,128)}, f32[1,1,3072]{2,1,0:T(1,128)S(1)}, u32[]{:S(2)}) copy-start(f32[1,1,3072]{2,1,0:T(1,128)S(1)} %get-tuple-element.106) | copy-start | bytes 36868
  15.5 12.5 %copy-start.7 = (f32[1,1,3072]{2,1,0:T(1,128)}, f32[1,1,3072]{2,1,0:T(1,128)S(1)}, u32[]{:S(2)}) copy-start(f32[1,1,3072]{2,1,0:T(1,128)S(1)} %get-tuple-element.107) | copy-start | bytes 36868
  15.5 12.5 %copy-start.9 = (f32[1,1,3072]{2,1,0:T(1,128)}, f32[1,1,3072]{2,1,0:T(1,128)S(1)}, u32[]{:S(2)}) copy-start(f32[1,1,3072]{2,1,0:T(1,128)S(1)} %get-tuple-element.108) | copy-start | bytes 36868
  15.5 12.5 %copy-start.11 = (f32[1,1,3072]{2,1,0:T(1,128)}, f32[1,1,3072]{2,1,0:T(1,128)S(1)}, u32[]{:S(2)}) copy-start(f32[1,1,3072]{2,1,0:T(1,128)S(1)} %get-tuple-element.109) | copy-start | bytes 36868
  15.5 12.5 %copy-start.13 = (f32[1,1,3072]{2,1,0:T(1,128)}, f32[1,1,3072]{2,1,0:T(1,128)S(1)}, u32[]{:S(2)}) copy-start(f32[1,1,3072]{2,1,0:T(1,128)S(1)} %get-tuple-element.110) | copy-start | bytes 36868
  15.5 12.5 %copy-start.15 = (f32[1,1,3072]{2,1,0:T(1,128)}, f32[1,1,3072]{2,1,0:T(1,128)S(1)}, u32[]{:S(2)}) copy-start(f32[1,1,3072]{2,1,0:T(1,128)S(1)} %get-tuple-element.111) | copy-start | bytes 36868
  15.5 12.5 %copy-start.17 = (f32[1,1,3072]{2,1,0:T(1,128)}, f32[1,1,3072]{2,1,0:T(1,128)S(1)}, u32[]{:S(2)}) copy-start(f32[1,1,3072]{2,1,0:T(1,128)S(1)} %get-tuple-element.112) | copy-start | bytes 36868
  15.5 12.5 %copy-start.19 = (f32[1,1,3072]{2,1,0:T(1,128)}, f32[1,1,3072]{2,1,0:T(1,128)S(1)}, u32[]{:S(2)}) copy-start(f32[1,1,3072]{2,1,0:T(1,128)S(1)} %get-tuple-element.113) | copy-start | bytes 36868
  15.6 12.5 %copy-start.21 = (f32[1,1,3072]{2,1,0:T(1,128)}, f32[1,1,3072]{2,1,0:T(1,128)S(1)}, u32[]{:S(2)}) copy-start(f32[1,1,3072]{2,1,0:T(1,128)S(1)} %get-tuple-element.114) | copy-start | bytes 36868
  15.6 12.5 %copy-start.23 = (f32[1,1,3072]{2,1,0:T(1,128)}, f32[1,1,3072]{2,1,0:T(1,128)S(1)}, u32[]{:S(2)}) copy-start(f32[1,1,3072]{2,1,0:T(1,128)S(1)} %get-tuple-element.115) | copy-start | bytes 36868
  15.6 12.5 %copy-start.25 = (f32[1,1,3072]{2,1,0:T(1,128)}, f32[1,1,3072]{2,1,0:T(1,128)S(1)}, u32[]{:S(2)}) copy-start(f32[1,1,3072]{2,1,0:T(1,128)S(1)} %get-tuple-element.116) | copy-start | bytes 36868
  17.9 10.2 %copy-start.27 = (f32[1,1,3072]{2,1,0:T(1,128)}, f32[1,1,3072]{2,1,0:T(1,128)S(1)}, u32[]{:S(2)}) copy-start(f32[1,1,3072]{2,1,0:T(1,128)S(1)} %get-tuple-element.68) | copy-start | bytes 36868
  17.9 10.2 %copy-start.29 = (f32[1,1,3072]{2,1,0:T(1,128)}, f32[1,1,3072]{2,1,0:T(1,128)S(1)}, u32[]{:S(2)}) copy-start(f32[1,1,3072]{2,1,0:T(1,128)S(1)} %get-tuple-element.69) | copy-start | bytes 36868
  17.9 10.2 %copy-start.31 = (f32[1,1,3072]{2,1,0:T(1,128)}, f32[1,1,3072]{2,1,0:T(1,128)S(1)}, u32[]{:S(2)}) copy-start(f32[1,1,3072]{2,1,0:T(1,128)S(1)} %get-tuple-element.70) | copy-start | bytes 36868
  22.7 45.5 %copy-start.88 = (f32[768]{0:T(1024)S(1)}, f32[768]{0:T(1024)}, u32[]{:S(2)}) copy-start(f32[768]{0:T(1024)} %param.17) | copy-start | bytes 9220
  29.5 80.2 %all-gather.3.cloned.1.call-start = ((), (), s32[]{:S(2)}) async-start(), calls=%async_computation.1 | async-start | bytes 1671168 | tf_op jit(solution)/shard_map/all_gather | solution.py:117
  30.3 155.1 %reduce-scatter.2.cloned.1.call-start = ((), (), s32[]{:S(2)}) async-start(), calls=%async_computation.3 | async-start | bytes 3342336 | tf_op jit(solution)/shard_map/reduce_scatter | solution.py:135
  120.1 167.8 %all-reduce.5.cloned.1.call-start = ((), (), s32[]{:S(2)}) async-start(), calls=%async_computation.4 | async-start | bytes 1376256 | tf_op jit(solution)/shard_map/psum | solution.py:159
  126.7 60.8 %copy-start.84 = (f32[4,4]{1,0:T(4,128)S(1)}, f32[4,4]{1,0:T(4,128)}, u32[]{:S(2)}) copy-start(f32[4,4]{1,0:T(4,128)} %copy-done.83) | copy-start | bytes 196
  191.7 65.4 %collective-permute-start.2 = (bf16[3,4,3072]{2,1,0:T(4,128)(2,1)S(1)}, bf16[3,4,3072]{2,1,0:T(4,128)(2,1)S(1)}, u32[]{:S(2)}, u32[]{:S(2)}) collective-permute-start(bf16[3,4,3072]{2,1,0:T(4,128)(2,1)S(1)} %get-tuple-element.118), channel_id=1, source_target_pairs={{0,1},{1,2},{2,3},{3,4},{4,5},{5,6},{6,7},{7,8},{8,9},{9,10},{10,1... | collective-permute-start | bytes 221192 | tf_op jit(solution)/shard_map/ppermute | solution.py:16
  191.8 65.3 %collective-permute-start.3 = (bf16[3,4,3072]{2,1,0:T(4,128)(2,1)S(1)}, bf16[3,4,3072]{2,1,0:T(4,128)(2,1)S(1)}, u32[]{:S(2)}, u32[]{:S(2)}) collective-permute-start(bf16[3,4,3072]{2,1,0:T(4,128)(2,1)S(1)} %get-tuple-element.119), channel_id=1, source_target_pairs={{1,0},{2,1},{3,2},{4,3},{5,4},{6,5},{7,6},{8,7},{9,8},{10,9},{11,1... | collective-permute-start | bytes 221192 | tf_op jit(solution)/shard_map/ppermute | solution.py:18
  196.4 61.6 %copy-start.6 = (f32[1,1,3072]{2,1,0:T(1,128)S(1)}, f32[1,1,3072]{2,1,0:T(1,128)}, u32[]{:S(2)}) copy-start(f32[1,1,3072]{2,1,0:T(1,128)} %copy-done.5) | copy-start | bytes 36868
  196.4 61.6 %copy-start.8 = (f32[1,1,3072]{2,1,0:T(1,128)S(1)}, f32[1,1,3072]{2,1,0:T(1,128)}, u32[]{:S(2)}) copy-start(f32[1,1,3072]{2,1,0:T(1,128)} %copy-done.7) | copy-start | bytes 36868
  196.4 61.6 %copy-start.10 = (f32[1,1,3072]{2,1,0:T(1,128)S(1)}, f32[1,1,3072]{2,1,0:T(1,128)}, u32[]{:S(2)}) copy-start(f32[1,1,3072]{2,1,0:T(1,128)} %copy-done.9) | copy-start | bytes 36868
  196.4 61.6 %copy-start.12 = (f32[1,1,3072]{2,1,0:T(1,128)S(1)}, f32[1,1,3072]{2,1,0:T(1,128)}, u32[]{:S(2)}) copy-start(f32[1,1,3072]{2,1,0:T(1,128)} %copy-done.11) | copy-start | bytes 36868
  196.4 61.6 %copy-start.14 = (f32[1,1,3072]{2,1,0:T(1,128)S(1)}, f32[1,1,3072]{2,1,0:T(1,128)}, u32[]{:S(2)}) copy-start(f32[1,1,3072]{2,1,0:T(1,128)} %copy-done.13) | copy-start | bytes 36868
  196.4 61.6 %copy-start.16 = (f32[1,1,3072]{2,1,0:T(1,128)S(1)}, f32[1,1,3072]{2,1,0:T(1,128)}, u32[]{:S(2)}) copy-start(f32[1,1,3072]{2,1,0:T(1,128)} %copy-done.15) | copy-start | bytes 36868
  196.4 61.6 %copy-start.18 = (f32[1,1,3072]{2,1,0:T(1,128)S(1)}, f32[1,1,3072]{2,1,0:T(1,128)}, u32[]{:S(2)}) copy-start(f32[1,1,3072]{2,1,0:T(1,128)} %copy-done.17) | copy-start | bytes 36868
  196.4 61.6 %copy-start.20 = (f32[1,1,3072]{2,1,0:T(1,128)S(1)}, f32[1,1,3072]{2,1,0:T(1,128)}, u32[]{:S(2)}) copy-start(f32[1,1,3072]{2,1,0:T(1,128)} %copy-done.19) | copy-start | bytes 36868
  196.4 61.6 %copy-start.22 = (f32[1,1,3072]{2,1,0:T(1,128)S(1)}, f32[1,1,3072]{2,1,0:T(1,128)}, u32[]{:S(2)}) copy-start(f32[1,1,3072]{2,1,0:T(1,128)} %copy-done.21) | copy-start | bytes 36868
  196.4 61.6 %copy-start.24 = (f32[1,1,3072]{2,1,0:T(1,128)S(1)}, f32[1,1,3072]{2,1,0:T(1,128)}, u32[]{:S(2)}) copy-start(f32[1,1,3072]{2,1,0:T(1,128)} %copy-done.23) | copy-start | bytes 36868
  196.5 61.6 %copy-start.26 = (f32[1,1,3072]{2,1,0:T(1,128)S(1)}, f32[1,1,3072]{2,1,0:T(1,128)}, u32[]{:S(2)}) copy-start(f32[1,1,3072]{2,1,0:T(1,128)} %copy-done.25) | copy-start | bytes 36868
  196.5 61.6 %copy-start.28 = (f32[1,1,3072]{2,1,0:T(1,128)S(1)}, f32[1,1,3072]{2,1,0:T(1,128)}, u32[]{:S(2)}) copy-start(f32[1,1,3072]{2,1,0:T(1,128)} %copy-done.27) | copy-start | bytes 36868
  196.5 61.6 %copy-start.30 = (f32[1,1,3072]{2,1,0:T(1,128)S(1)}, f32[1,1,3072]{2,1,0:T(1,128)}, u32[]{:S(2)}) copy-start(f32[1,1,3072]{2,1,0:T(1,128)} %copy-done.29) | copy-start | bytes 36868
  196.5 61.6 %copy-start.32 = (f32[1,1,3072]{2,1,0:T(1,128)S(1)}, f32[1,1,3072]{2,1,0:T(1,128)}, u32[]{:S(2)}) copy-start(f32[1,1,3072]{2,1,0:T(1,128)} %copy-done.31) | copy-start | bytes 36868
  196.5 61.6 %copy-start.34 = (f32[1,1,3072]{2,1,0:T(1,128)S(1)}, f32[1,1,3072]{2,1,0:T(1,128)}, u32[]{:S(2)}) copy-start(f32[1,1,3072]{2,1,0:T(1,128)} %copy-done.33) | copy-start | bytes 36868
  196.5 61.6 %copy-start.36 = (f32[1,1,3072]{2,1,0:T(1,128)S(1)}, f32[1,1,3072]{2,1,0:T(1,128)}, u32[]{:S(2)}) copy-start(f32[1,1,3072]{2,1,0:T(1,128)} %copy-done.35) | copy-start | bytes 36868
  196.5 61.6 %copy-start.38 = (f32[1,1,3072]{2,1,0:T(1,128)S(1)}, f32[1,1,3072]{2,1,0:T(1,128)}, u32[]{:S(2)}) copy-start(f32[1,1,3072]{2,1,0:T(1,128)} %copy-done.37) | copy-start | bytes 36868
  196.5 61.6 %copy-start.40 = (f32[1,1,3072]{2,1,0:T(1,128)S(1)}, f32[1,1,3072]{2,1,0:T(1,128)}, u32[]{:S(2)}) copy-start(f32[1,1,3072]{2,1,0:T(1,128)} %copy-done.39) | copy-start | bytes 36868
  196.5 61.6 %copy-start.42 = (f32[1,1,3072]{2,1,0:T(1,128)S(1)}, f32[1,1,3072]{2,1,0:T(1,128)}, u32[]{:S(2)}) copy-start(f32[1,1,3072]{2,1,0:T(1,128)} %copy-done.41) | copy-start | bytes 36868
  196.5 61.6 %copy-start.44 = (f32[1,1,3072]{2,1,0:T(1,128)S(1)}, f32[1,1,3072]{2,1,0:T(1,128)}, u32[]{:S(2)}) copy-start(f32[1,1,3072]{2,1,0:T(1,128)} %copy-done.43) | copy-start | bytes 36868
  196.6 61.6 %copy-start.46 = (f32[1,1,3072]{2,1,0:T(1,128)S(1)}, f32[1,1,3072]{2,1,0:T(1,128)}, u32[]{:S(2)}) copy-start(f32[1,1,3072]{2,1,0:T(1,128)} %copy-done.45) | copy-start | bytes 36868
  196.6 61.6 %copy-start.48 = (f32[1,1,3072]{2,1,0:T(1,128)S(1)}, f32[1,1,3072]{2,1,0:T(1,128)}, u32[]{:S(2)}) copy-start(f32[1,1,3072]{2,1,0:T(1,128)} %copy-done.47) | copy-start | bytes 36868
  196.6 61.6 %copy-start.50 = (f32[1,1,3072]{2,1,0:T(1,128)S(1)}, f32[1,1,3072]{2,1,0:T(1,128)}, u32[]{:S(2)}) copy-start(f32[1,1,3072]{2,1,0:T(1,128)} %copy-done.49) | copy-start | bytes 36868
  196.6 61.6 %copy-start.52 = (f32[1,1,3072]{2,1,0:T(1,128)S(1)}, f32[1,1,3072]{2,1,0:T(1,128)}, u32[]{:S(2)}) copy-start(f32[1,1,3072]{2,1,0:T(1,128)} %copy-done.51) | copy-start | bytes 36868
  196.6 61.6 %copy-start.54 = (f32[1,1,3072]{2,1,0:T(1,128)S(1)}, f32[1,1,3072]{2,1,0:T(1,128)}, u32[]{:S(2)}) copy-start(f32[1,1,3072]{2,1,0:T(1,128)} %copy-done.53) | copy-start | bytes 36868
  196.6 61.6 %copy-start.56 = (f32[1,1,3072]{2,1,0:T(1,128)S(1)}, f32[1,1,3072]{2,1,0:T(1,128)}, u32[]{:S(2)}) copy-start(f32[1,1,3072]{2,1,0:T(1,128)} %copy-done.55) | copy-start | bytes 36868
  196.6 61.6 %copy-start.58 = (f32[1,1,3072]{2,1,0:T(1,128)S(1)}, f32[1,1,3072]{2,1,0:T(1,128)}, u32[]{:S(2)}) copy-start(f32[1,1,3072]{2,1,0:T(1,128)} %copy-done.57) | copy-start | bytes 36868
  196.6 61.6 %copy-start.60 = (f32[1,1,3072]{2,1,0:T(1,128)S(1)}, f32[1,1,3072]{2,1,0:T(1,128)}, u32[]{:S(2)}) copy-start(f32[1,1,3072]{2,1,0:T(1,128)} %copy-done.59) | copy-start | bytes 36868
  196.6 61.6 %copy-start.62 = (f32[1,1,3072]{2,1,0:T(1,128)S(1)}, f32[1,1,3072]{2,1,0:T(1,128)}, u32[]{:S(2)}) copy-start(f32[1,1,3072]{2,1,0:T(1,128)} %copy-done.61) | copy-start | bytes 36868
  196.6 61.6 %copy-start.64 = (f32[1,1,3072]{2,1,0:T(1,128)S(1)}, f32[1,1,3072]{2,1,0:T(1,128)}, u32[]{:S(2)}) copy-start(f32[1,1,3072]{2,1,0:T(1,128)} %copy-done.63) | copy-start | bytes 36868
  196.7 61.6 %copy-start.66 = (f32[1,1,3072]{2,1,0:T(1,128)S(1)}, f32[1,1,3072]{2,1,0:T(1,128)}, u32[]{:S(2)}) copy-start(f32[1,1,3072]{2,1,0:T(1,128)} %copy-done.65) | copy-start | bytes 36868
  196.7 61.6 %copy-start.68 = (f32[1,1,3072]{2,1,0:T(1,128)S(1)}, f32[1,1,3072]{2,1,0:T(1,128)}, u32[]{:S(2)}) copy-start(f32[1,1,3072]{2,1,0:T(1,128)} %copy-done.67) | copy-start | bytes 36868
  196.7 61.6 %copy-start.70 = (f32[1,1,3072]{2,1,0:T(1,128)S(1)}, f32[1,1,3072]{2,1,0:T(1,128)}, u32[]{:S(2)}) copy-start(f32[1,1,3072]{2,1,0:T(1,128)} %copy-done.69) | copy-start | bytes 36868
  196.7 61.6 %copy-start.72 = (f32[1,1,3072]{2,1,0:T(1,128)S(1)}, f32[1,1,3072]{2,1,0:T(1,128)}, u32[]{:S(2)}) copy-start(f32[1,1,3072]{2,1,0:T(1,128)} %copy-done.71) | copy-start | bytes 36868
  196.7 61.6 %copy-start.74 = (f32[1,1,3072]{2,1,0:T(1,128)S(1)}, f32[1,1,3072]{2,1,0:T(1,128)}, u32[]{:S(2)}) copy-start(f32[1,1,3072]{2,1,0:T(1,128)} %copy-done.73) | copy-start | bytes 36868
  196.7 61.6 %copy-start.76 = (f32[1,1,3072]{2,1,0:T(1,128)S(1)}, f32[1,1,3072]{2,1,0:T(1,128)}, u32[]{:S(2)}) copy-start(f32[1,1,3072]{2,1,0:T(1,128)} %copy-done.75) | copy-start | bytes 36868
  196.7 61.6 %copy-start.78 = (f32[1,1,3072]{2,1,0:T(1,128)S(1)}, f32[1,1,3072]{2,1,0:T(1,128)}, u32[]{:S(2)}) copy-start(f32[1,1,3072]{2,1,0:T(1,128)} %copy-done.77) | copy-start | bytes 36868
  196.7 61.6 %copy-start.80 = (f32[1,1,3072]{2,1,0:T(1,128)S(1)}, f32[1,1,3072]{2,1,0:T(1,128)}, u32[]{:S(2)}) copy-start(f32[1,1,3072]{2,1,0:T(1,128)} %copy-done.79) | copy-start | bytes 36868
  196.7 61.6 %copy-start.82 = (f32[1,1,3072]{2,1,0:T(1,128)S(1)}, f32[1,1,3072]{2,1,0:T(1,128)}, u32[]{:S(2)}) copy-start(f32[1,1,3072]{2,1,0:T(1,128)} %copy-done.81) | copy-start | bytes 36868
  (33 other events, 271.5 us)
Sparse Core Ops, SparseCore 0:
  29.6 38.5 all-gather.4
  71.1 38.5 all-gather.2
  120.2 65.0 reduce-scatter.1
  198.7 89.1 all-reduce.4
where the time goes:
time: 297 us; the launch traced here: 296 us
  waiting for transfers between devices  154 us (52%)
  blocking collectives  58.5 us (20%)
  matrix products  25 us (8%)
  other arithmetic  17.7 us (6%)
  local copies, waits for them, and re-layouts  15.6 us (5%)
  between operations  15.3 us (5%)
  starting transfers between devices  10.4 us (4%)
    psum x1, blocking collectives, on_device(): lax.psum((gain_part, shift_part, kernel_part, bias_part), 'rows')  58.5 us
    reduce_scatter x1, waiting for transfers between devices, on_device(): lax.psum_scatter(contract(act_grad, up_weight, 1, 1), 'rows', scatter_dim...  53.5 us
    all_gather x1, waiting for transfers between devices, on_device(): normed_all = lax.all_gather(normed, 'rows', axis=0, tiled=True)  37.9 us
    all_gather x1, waiting for transfers between devices, on_device(): cot_all = lax.all_gather(cot_scaled, 'rows', axis=0, tiled=True)  37.2 us
    psum x1, waiting for transfers between devices, on_device(): lax.psum((gain_part, shift_part, kernel_part, bias_part), 'rows')  25.3 us
    dot_general x4, matrix products, contract(): lax.dot_general(left, right, (((left_dim,), (right_dim,)), ((), ())), pre...  20.8 us
    ppermute x2, starting transfers between devices, extended(): lax.ppermute(head, axis, [((i + 1) % count, i) for i in range(count)])  9.49 us
  transfers between devices with their start and end apart: 8, of which 4 were waited for; matrix products, arithmetic and copies ran while one was open for 10% of the time, Pallas kernels for 0%

commit v1 on v0

--- a/solution.py
+++ b/solution.py
@@ -114,7 +114,6 @@
         .astype(jnp.bfloat16)
         .reshape(rows_dev * col_count, channels)
     )
-    cot_all = lax.all_gather(cot_scaled, "rows", axis=0, tiled=True)
     near_rows = extended(features, (("rows", 0),), 3)
     padded = pad_columns(near_rows.astype(jnp.float32) * row_mask)
     conv_out = depthwise(padded, depth_kernel, depth_bias, rows_dev, col_count)
@@ -124,7 +123,11 @@
         .astype(jnp.bfloat16)
         .reshape(rows_dev * col_count, channels)
     )
-    normed_all = lax.all_gather(normed, "rows", axis=0, tiled=True)
+    cot_all, normed_all = jnp.split(
+        lax.all_gather(jnp.concatenate([cot_scaled, normed], axis=1), "rows", axis=0, tiled=True),
+        [cot_scaled.shape[1]],
+        axis=1,
+    )
     pre_act = jnp.dot(normed_all, up_weight, preferred_element_type=jnp.float32) + up_bias
     hidden = gelu_value(pre_act).astype(jnp.bfloat16)
     down_grad = contract(hidden, cot_all, 0, 0)

time: 297 us -> 260 us (0.88)
  waiting for transfers between devices: 154 us -> 125 us
  local copies, waits for them, and re-layouts: 15.6 us -> 12.2 us
    all_gather x2 -> x1, waiting for transfers between devices: 75.1 us -> 44.2 us  [on_device(): lax.all_gather(jnp.concatenate([cot_scaled, normed], axis=1), 'rows', axi...]
  transfers between devices with their start and end apart: 8 -> 7, of which waited for: 4 -> 3; matrix products, arithmetic and copies ran while one was open for 10% -> 9% of each run, Pallas kernels for 0% -> 0%
where the time goes in v1:
time: 260 us; the launch traced here: 259 us
  waiting for transfers between devices  125 us (48%)
  blocking collectives  58.5 us (22%)
  matrix products  24 us (9%)
  other arithmetic  15.3 us (6%)
  between operations  14.1 us (5%)
  local copies, waits for them, and re-layouts  12.2 us (5%)
  starting transfers between devices  10.4 us (4%)
    psum x1, blocking collectives, on_device(): lax.psum((gain_part, shift_part, kernel_part, bias_part), 'rows')  58.5 us
    reduce_scatter x1, waiting for transfers between devices, on_device(): lax.psum_scatter(contract(act_grad, up_weight, 1, 1), 'rows', scatter_dim...  53 us
    all_gather x1, waiting for transfers between devices, on_device(): lax.all_gather(jnp.concatenate([cot_scaled, normed], axis=1), 'rows', axi...  44.2 us
    psum x1, waiting for transfers between devices, on_device(): lax.psum((gain_part, shift_part, kernel_part, bias_part), 'rows')  27.4 us
    dot_general x4, matrix products, contract(): lax.dot_general(left, right, (((left_dim,), (right_dim,)), ((), ())), pre...  19.7 us
    ppermute x2, starting transfers between devices, extended(): lax.ppermute(head, axis, [((i + 1) % count, i) for i in range(count)])  9.49 us
  transfers between devices with their start and end apart: 7, of which 3 were waited for; matrix products, arithmetic and copies ran while one was open for 9% of the time, Pallas kernels for 0%

profile of v1, /device:TPU:0, one launch (start us, length us, event | category | flops | bytes accessed | tf_op | source)
XLA Modules:
  0.0 259.1 jit_solution(12837360268014230585)
XLA Ops:
  7.2 0.0 copy-start.3
  7.2 0.0 copy-start.6
  7.2 0.0 all-gather.2.cloned.1.call-start
  7.2 1.0 fusion.122
  8.3 0.5 collective-permute-start
  8.8 5.1 %collective-permute-start.1 = (bf16[3,4,3072]{2,1,0:T(4,128)(2,1)S(1)}, bf16[3,4,3072]{2,1,0:T(4,128)(2,1)S(1)}, u32[]{:S(2)}, u32[]{:S(2)}) collective-permute-start(bf16[3,4,3072]{2,1,0:T(4,128)(2,1)S(1)} %get-tuple-element.121), channel_id=1, source_target_pairs={{1,0},{2,1},{3,2},{4,3},{5,4},{6,5},{7,6},{8,7},{9,8},{10,9},{11,1... | collective-permute-start | bytes 221192 | tf_op jit(solution)/shard_map/ppermute | solution.py:18
  13.8 1.7 fusion.120
  15.5 2.3 fusion.118
  17.8 2.1 fusion.119
  19.9 0.9 fusion.22
  20.9 0.0 copy-start.5
  20.9 0.0 copy-start.7
  21.0 0.0 collective-permute-done
  21.0 0.0 collective-permute-done.1
  21.0 0.0 copy-done.3
  21.0 0.2 convert_multiply_fusion.1
  21.2 0.0 copy-done.6
  21.2 0.0 copy-start.8
  21.2 4.4 %fusion.117 = (f32[4,4]{1,0:T(4,128)S(1)}, f32[4,4,3072]{2,1,0:T(4,128)S(1)}) fusion(f32[3072]{0:T(1024)S(1)} %copy-done.6, f32[3072]{0:T(1024)S(1)} %bitcast.137, f32[3072]{0:T(1024)S(1)} %bitcast.139, f32[3072]{0:T(1024)S(1)} %bitcast.143, f32[10,4,3072]{2,1,0:T(4,128)S(1)} %convert_multiply_fusion.1, f32[3072]{0:T(1024)S(1)} %bitcast.145, ...), kind=kLoop, calls=%fused_computation.287 | loop fusion | flops 4866032 | bytes 2678848 | tf_op jit(solution)/shard_map/reduce_sum | solution.py:72
  25.6 0.2 multiply_reduce_fusion.52
  25.8 0.0 copy-done.5
  25.9 0.1 add_convert_fusion
  26.0 0.7 pad_maximum_fusion
  26.7 0.0 all-gather.2.cloned.1.call-update
  26.7 0.0 reduce-scatter.2.cloned.1.call-start
  26.8 44.2 %all-gather.2.cloned.1.call-done = bf16[256,6144]{1,0:T(8,128)(2,1)} async-done(((bf16[16,6144]{1,0:T(8,128)(2,1)}), bf16[256,6144]{1,0:T(8,128)(2,1)}) %all-gather.2.cloned.1.call-update) | async-done | bytes 3145744 | tf_op jit(solution)/shard_map/all_gather | solution.py:127
  71.0 0.0 copy-done.8
  71.0 4.3 %fusion.11 = f32[256,768]{1,0:T(8,128)S(1)} fusion(bf16[3072,768]{1,0:T(8,128)(2,1)} %param.16, bf16[256,6144]{1,0:T(8,128)(2,1)} %all-gather.2.cloned.1.call-done, f32[768]{0:T(1024)S(1)} %copy-done.8), kind=kOutput, calls=%fused_computation.93 | convolution fusion | flops 1208156160 | bytes 7080960 | tf_op jit(solution)/shard_map/dot_general | solution.py:131
  75.4 0.0 slice-start.1
  75.4 4.6 %convert_reduce_fusion = (f32[768]{0:T(1024)}, bf16[256,768]{1,0:T(8,128)(2,1)S(1)}) fusion(f32[256,768]{1,0:T(8,128)S(1)} %fusion.11, bf16[768,3072]{1,0:T(8,128)(2,1)} %param.18, bf16[256,6144]{1,0:T(8,128)(2,1)S(1)} %copy-done), kind=kOutput, calls=%fused_computation.101 | convolution fusion | flops 1210318080 | bytes 7474176 | tf_op jit(solution)/shard_map/dot_general | solution.py:35
  80.0 3.2 %fusion.123 = f32[256,3072]{1,0:T(8,128)} fusion(bf16[256,768]{1,0:T(8,128)(2,1)S(1)} %get-tuple-element.123, bf16[3072,768]{1,0:T(8,128)(2,1)S(1)} %bitcast.118), kind=kOutput, calls=%fused_computation.293 | convolution fusion | flops 1207959552 | bytes 8257536 | tf_op jit(solution)/shard_map/dot_general | solution.py:35
  83.1 0.0 reduce-scatter.2.cloned.1.call-update
  83.1 0.2 all-reduce.5.cloned.1.call-start
  83.4 6.7 %fusion = f32[3072,768]{1,0:T(8,128)} fusion(bf16[256,768]{1,0:T(8,128)(2,1)S(1)} %get-tuple-element.123, bf16[256,6144]{1,0:T(8,128)(2,1)} %all-gather.2.cloned.1.call-done), kind=kOutput, calls=%fused_computation.84 | convolution fusion | flops 1207959552 | bytes 11403264 | tf_op jit(solution)/shard_map/dot_general | solution.py:35
  90.1 0.0 copy-done.1
  90.1 5.2 %fusion.4 = f32[768,3072]{1,0:T(8,128)} fusion(bf16[256,6144]{1,0:T(8,128)(2,1)S(1)} %copy-done.1, f32[256,768]{1,0:T(8,128)S(1)} %fusion.11), kind=kOutput, calls=%fused_computation.88 | convolution fusion | flops 1208942592 | bytes 11796480 | tf_op jit(solution)/shard_map/dot_general | solution.py:35
  95.3 53.0 %reduce-scatter.2.cloned.1.call-done = f32[16,3072]{1,0:T(8,128)} async-done(((f32[256,3072]{1,0:T(8,128)}), f32[16,3072]{1,0:T(8,128)}) %reduce-scatter.2.cloned.1.call-update) | async-done | bytes 196624 | tf_op jit(solution)/shard_map/reduce_scatter | solution.py:138
  148.3 1.1 fusion.116
  149.4 0.1 div.44
  149.5 1.0 reshape.91
  150.5 0.3 multiply_reduce_fusion
  150.7 1.5 multiply_reduce_fusion.1
  152.2 1.0 multiply_reduce_fusion.37
  153.3 1.3 multiply_reduce_fusion.19
  154.7 0.1 collective-permute-start.2
  154.7 4.4 %collective-permute-start.3 = (bf16[3,4,3072]{2,1,0:T(4,128)(2,1)S(1)}, bf16[3,4,3072]{2,1,0:T(4,128)(2,1)S(1)}, u32[]{:S(2)}, u32[]{:S(2)}) collective-permute-start(bf16[3,4,3072]{2,1,0:T(4,128)(2,1)S(1)} %get-tuple-element.119), channel_id=1, source_target_pairs={{1,0},{2,1},{3,2},{4,3},{5,4},{6,5},{7,6},{8,7},{9,8},{10,9},{11,1... | collective-permute-start | bytes 221192 | tf_op jit(solution)/shard_map/ppermute | solution.py:18
  159.2 0.1 stack.199
  159.3 0.0 copy-start.4
  159.3 0.1 stack.208
  159.5 0.1 stack.217
  159.6 0.1 stack.226
  159.8 0.1 stack.235
  160.0 0.1 stack.244
  160.1 0.1 stack.253
  160.3 0.0 copy-start.2
  160.3 0.8 copy-done.2
  161.1 0.0 all-reduce.5.cloned.1.call-update
  161.2 58.5 %all-reduce.2 = (f32[3072]{0:T(1024)}, f32[3072]{0:T(1024)}, f32[3072]{0:T(1024)}) all-reduce(f32[3072]{0:T(1024)S(1)} %get-tuple-element.61, f32[3072]{0:T(1024)S(1)} %get-tuple-element.57, f32[3072]{0:T(1024)S(1)} %get-tuple-element.59), channel_id=1, replica_groups=mesh['groups'=2,'rows'=16] {'rows'}, use_global_device_ids=true, to_apply=%region_57.58 | all-reduce | flops 9216 | bytes 73728 | tf_op jit(solution)/shard_map/psum | solution.py:162
  219.7 0.0 collective-permute-done.2
  219.7 0.0 collective-permute-done.3
  219.7 0.2 convert_multiply_fusion
  219.9 3.3 %fusion.23 = bf16[4,4,3072]{2,1,0:T(4,128)(2,1)} fusion(bf16[4,4,3072]{2,1,0:T(4,128)(2,1)S(1)} %copy-done.4, f32[10,4,3072]{2,1,0:T(4,128)S(1)} %convert_multiply_fusion, f32[3072]{0:T(1024)S(1)} %bitcast.138, f32[3072]{0:T(1024)S(1)} %bitcast.140, f32[3072]{0:T(1024)S(1)} %bitcast.144, f32[3072]{0:T(1024)S(1)} %bitcast.146, f32[3072]{0:T(1024)S(1)} %bitcast.148, ...), kind=kLoop, calls=%fused_computation.109 | loop fusion | flops 4915200 | bytes 2666496 | tf_op jit(solution)/shard_map/convert_element_type | solution.py:161
  223.2 27.4 %all-reduce.5.cloned.1.call-done = f32[7,7,3072]{2,1,0:T(8,128)} async-done(((f32[7,7,3072]{2,1,0:T(8,128)}), f32[7,7,3072]{2,1,0:T(8,128)}) %all-reduce.5.cloned.1.call-update) | async-done | bytes 602128 | tf_op jit(solution)/shard_map/psum | solution.py:162
  250.6 2.0 copy.25
  (24 shorter events, 0.2 us)
Async XLA Ops:
  7.2 13.8 %copy-start.3 = (bf16[4,4,3072]{2,1,0:T(4,128)(2,1)S(1)}, bf16[4,4,3072]{2,1,0:T(4,128)(2,1)}, u32[]{:S(2)}) copy-start(bf16[4,4,3072]{2,1,0:T(4,128)(2,1)} %param.10) | copy-start | bytes 294916
  7.2 14.0 %copy-start.6 = (f32[3072]{0:T(1024)S(1)}, f32[3072]{0:T(1024)}, u32[]{:S(2)}) copy-start(f32[3072]{0:T(1024)} %param.13) | copy-start | bytes 36868
  7.2 63.8 %all-gather.2.cloned.1.call-start = ((), (), s32[]{:S(2)}) async-start(), calls=%async_computation.1 | async-start | bytes 3342336 | tf_op jit(solution)/shard_map/all_gather | solution.py:127
  8.3 12.7 %collective-permute-start = (bf16[3,4,3072]{2,1,0:T(4,128)(2,1)S(1)}, bf16[3,4,3072]{2,1,0:T(4,128)(2,1)S(1)}, u32[]{:S(2)}, u32[]{:S(2)}) collective-permute-start(bf16[3,4,3072]{2,1,0:T(4,128)(2,1)S(1)} %get-tuple-element.120), channel_id=1, source_target_pairs={{0,1},{1,2},{2,3},{3,4},{4,5},{5,6},{6,7},{7,8},{8,9},{9,10},{10,1... | collective-permute-start | bytes 221192 | tf_op jit(solution)/shard_map/ppermute | solution.py:16
  8.8 12.2 %collective-permute-start.1 = (bf16[3,4,3072]{2,1,0:T(4,128)(2,1)S(1)}, bf16[3,4,3072]{2,1,0:T(4,128)(2,1)S(1)}, u32[]{:S(2)}, u32[]{:S(2)}) collective-permute-start(bf16[3,4,3072]{2,1,0:T(4,128)(2,1)S(1)} %get-tuple-element.121), channel_id=1, source_target_pairs={{1,0},{2,1},{3,2},{4,3},{5,4},{6,5},{7,6},{8,7},{9,8},{10,9},{11,1... | collective-permute-start | bytes 221192 | tf_op jit(solution)/shard_map/ppermute | solution.py:18
  20.9 5.0 %copy-start.5 = (f32[3072]{0:T(1024)S(1)}, f32[3072]{0:T(1024)}, u32[]{:S(2)}) copy-start(f32[3072]{0:T(1024)} %param.14) | copy-start | bytes 36868
  20.9 4.9 %copy-start.7 = (f32[3072]{0:T(1024)S(1)}, f32[3072]{0:T(1024)}, u32[]{:S(2)}) copy-start(f32[3072]{0:T(1024)} %param.15) | copy-start | bytes 36868
  21.2 49.8 %copy-start.8 = (f32[768]{0:T(1024)S(1)}, f32[768]{0:T(1024)}, u32[]{:S(2)}) copy-start(f32[768]{0:T(1024)} %param.17) | copy-start | bytes 9220
  26.7 121.6 %reduce-scatter.2.cloned.1.call-start = ((), (), s32[]{:S(2)}) async-start(), calls=%async_computation.2 | async-start | bytes 3342336 | tf_op jit(solution)/shard_map/reduce_scatter | solution.py:138
  71.0 4.3 %copy-start = (bf16[256,6144]{1,0:T(8,128)(2,1)S(1)}, bf16[256,6144]{1,0:T(8,128)(2,1)}, u32[]{:S(2)}) copy-start(bf16[256,6144]{1,0:T(8,128)(2,1)} %all-gather.2.cloned.1.call-done) | copy-start | bytes 9437188
  71.0 8.9 %slice-start = ((s8[4718592]{0:T(1024)(128)(4,1)}), s8[4194304]{0:T(1024)(128)(4,1)S(1)}, s32[]{:S(2)}) async-start(s8[4718592]{0:T(1024)(128)(4,1)} %bitcast.117), calls=%async_computation.4 | async-start | bytes 8388608
  75.4 4.6 %slice-start.1 = ((s8[4718592]{0:T(1024)(128)(4,1)}), s8[524288]{0:T(1024)(128)(4,1)S(1)}, s32[]{:S(2)}) async-start(s8[4718592]{0:T(1024)(128)(4,1)} %bitcast.117), calls=%async_computation.5 | async-start | bytes 1048576
  83.1 167.5 %all-reduce.5.cloned.1.call-start = ((), (), s32[]{:S(2)}) async-start(), calls=%async_computation.3 | async-start | bytes 1376256 | tf_op jit(solution)/shard_map/psum | solution.py:162
  83.4 6.8 %copy-start.1 = (bf16[256,6144]{1,0:T(8,128)(2,1)S(1)}, bf16[256,6144]{1,0:T(8,128)(2,1)}, u32[]{:S(2)}) copy-start(bf16[256,6144]{1,0:T(8,128)(2,1)} %all-gather.2.cloned.1.call-done) | copy-start | bytes 9437188
  154.7 65.0 %collective-permute-start.2 = (bf16[3,4,3072]{2,1,0:T(4,128)(2,1)S(1)}, bf16[3,4,3072]{2,1,0:T(4,128)(2,1)S(1)}, u32[]{:S(2)}, u32[]{:S(2)}) collective-permute-start(bf16[3,4,3072]{2,1,0:T(4,128)(2,1)S(1)} %get-tuple-element.118), channel_id=1, source_target_pairs={{0,1},{1,2},{2,3},{3,4},{4,5},{5,6},{6,7},{7,8},{8,9},{9,10},{10,1... | collective-permute-start | bytes 221192 | tf_op jit(solution)/shard_map/ppermute | solution.py:16
  154.7 64.9 %collective-permute-start.3 = (bf16[3,4,3072]{2,1,0:T(4,128)(2,1)S(1)}, bf16[3,4,3072]{2,1,0:T(4,128)(2,1)S(1)}, u32[]{:S(2)}, u32[]{:S(2)}) collective-permute-start(bf16[3,4,3072]{2,1,0:T(4,128)(2,1)S(1)} %get-tuple-element.119), channel_id=1, source_target_pairs={{1,0},{2,1},{3,2},{4,3},{5,4},{6,5},{7,6},{8,7},{9,8},{10,9},{11,1... | collective-permute-start | bytes 221192 | tf_op jit(solution)/shard_map/ppermute | solution.py:18
  159.3 60.6 %copy-start.4 = (bf16[4,4,3072]{2,1,0:T(4,128)(2,1)S(1)}, bf16[4,4,3072]{2,1,0:T(4,128)(2,1)}, u32[]{:S(2)}) copy-start(bf16[4,4,3072]{2,1,0:T(4,128)(2,1)} %param.11) | copy-start | bytes 294916
  160.3 0.8 copy-start.2
Sparse Core Ops, SparseCore 0:
  26.9 44.1 all-gather.1
  83.3 65.0 reduce-scatter.1
  161.3 89.2 all-reduce.4
